TPU v7x, 256 devices: a whole 4x4x8 slice. The times are simulated.
256 devices in a mesh: rep: 8 (over x, y_hi), fsdp: 32 (over z, y_lo, core).
Axes of the slice: x: 4, y: 4 (y_hi: 2, y_lo: 2; y = y_hi * 2 + y_lo), z: 8, core: 2. Of those that a mesh axis runs over, the one named last changes fastest.
Arguments:
- tokens: bfloat16 [8, 2048, 2048], P('rep', 'fsdp'), may hold values from -6 to 6
- cotangent: bfloat16 [8, 2048, 2048], P('rep', 'fsdp'), may hold values from -6 to 6
- gain: float32 [8, 2048], P('rep'), may hold values from 0.1 to 1.9
- w_gate: float32 [8, 2048, 4096], P('rep', None, 'fsdp'), may hold values from -5 to 5
- w_up: float32 [8, 2048, 4096], P('rep', None, 'fsdp'), may hold values from -5 to 5
- w_down: float32 [8, 4096, 2048], P('rep', 'fsdp'), may hold values from -5 to 5
- step_index: int32 [1], replicated, may hold values from 0 to 999
Outputs:
- input_grad: bfloat16 [8, 2048, 2048], P('rep', 'fsdp')
- new_gain: float32 [8, 2048], P('rep')
- new_gate: float32 [8, 2048, 4096], P('rep', None, 'fsdp')
- new_up: float32 [8, 2048, 4096], P('rep', None, 'fsdp')
- new_down: float32 [8, 4096, 2048], P('rep', 'fsdp')
All inputs are finite; a program needn't handle non-finite values.
Results may differ from a plain program's by a relative error of at most 0.025.
Values may be sent and summed in bfloat16 or wider, within the bound.
A program may use at most 128 MiB of HBM per device.

v0:
```python
import jax
import jax.numpy as jnp
from jax import lax
from jax.sharding import PartitionSpec as P

learn_rate = 0.02
epsilon = 1e-05


def for_sending(x):
    return jax.tree.map(lambda a: a.astype(jnp.bfloat16) if a.dtype == jnp.float32 else a, x)


def from_partner(x, axis, distance):
    return lax.ppermute(x, axis, [(i, i ^ 1 << distance) for i in range(lax.axis_size(axis))])


def swap_together(values, bit_pos):
    return tuple(
        (
            jax.tree.map(
                lambda part, own: part.astype(own.dtype),
                from_partner(for_sending(member), "rep", bit_pos),
                member,
            )
            for member in values
        )
    )


def partner_average(values, step_index, swap_helper):
    level_count = lax.axis_size("rep").bit_length() - 1
    branches = [
        lambda members, bit_pos=bit_pos: swap_helper(members, bit_pos)
        for bit_pos in range(level_count)
    ]
    received = lax.switch(step_index[0] % level_count, branches, values)
    return tuple((0.5 * (mine + theirs) for mine, theirs in zip(values, received)))


def local(tokens, cotangent, gain, w_gate, w_up, w_down, step_index):
    own_rows = tokens[0]
    model_width = own_rows.shape[1]
    local_units = w_gate.shape[2]
    in_scale = model_width ** (-0.5)
    out_scale = (local_units * lax.axis_size("fsdp")) ** (-0.5)
    values = own_rows.astype(jnp.float32)
    inv_rms = lax.rsqrt(jnp.mean(values * values, axis=1, keepdims=True) + epsilon)
    unit_rows = values * inv_rms
    gain_row = gain[0]
    normed = (unit_rows * gain_row).astype(jnp.bfloat16)
    both_weights = jnp.concatenate([w_gate[0], w_up[0]], axis=1).astype(jnp.bfloat16)
    down_b = w_down[0].astype(jnp.bfloat16)
    gathered = lax.all_gather(normed, "fsdp", axis=0, tiled=True)
    both_pre = jnp.dot(gathered, both_weights, preferred_element_type=jnp.float32) * in_scale
    gate_pre = both_pre[:, :local_units]
    up_pre = both_pre[:, local_units:]
    sigmoid_gate = jax.nn.sigmoid(gate_pre)
    activated = gate_pre * sigmoid_gate
    hidden = (activated * up_pre).astype(jnp.bfloat16)
    grad_all = lax.all_gather(cotangent[0], "fsdp", axis=0, tiled=True)
    grad_down = (
        lax.dot_general(
            hidden, grad_all, (((0,), (0,)), ((), ())), preferred_element_type=jnp.float32
        )
        * out_scale
    )
    new_down = w_down[0] - learn_rate * grad_down
    grad_hidden = (
        lax.dot_general(
            grad_all, down_b, (((1,), (1,)), ((), ())), preferred_element_type=jnp.float32
        )
        * out_scale
    )
    grad_gate = grad_hidden * up_pre * sigmoid_gate * (1.0 + gate_pre * (1.0 - sigmoid_gate))
    grad_up = grad_hidden * activated
    grad_both = jnp.concatenate(
        [grad_gate.astype(jnp.bfloat16), grad_up.astype(jnp.bfloat16)], axis=1
    )
    grad_weights = (
        lax.dot_general(
            gathered, grad_both, (((0,), (0,)), ((), ())), preferred_element_type=jnp.float32
        )
        * in_scale
    )
    grad_normed = lax.psum_scatter(
        (
            lax.dot_general(
                grad_both,
                both_weights,
                (((1,), (1,)), ((), ())),
                preferred_element_type=jnp.float32,
            )
            * in_scale
        ).astype(jnp.bfloat16),
        "fsdp",
        scatter_dimension=0,
        tiled=True,
    ).astype(jnp.float32)
    grad_gain = lax.psum(jnp.sum(grad_normed * unit_rows, axis=0), "fsdp")
    scaled = grad_normed * gain_row
    input_grad = cotangent[0].astype(jnp.float32) + inv_rms * (
        scaled - unit_rows * jnp.mean(scaled * unit_rows, axis=1, keepdims=True)
    )
    input_grad = input_grad.astype(jnp.bfloat16)
    new_gain = gain_row - learn_rate * grad_gain
    new_gate = w_gate[0] - learn_rate * grad_weights[:, :local_units]
    new_up = w_up[0] - learn_rate * grad_weights[:, local_units:]
    new_gain, new_gate, new_up, new_down = partner_average(
        (new_gain, new_gate, new_up, new_down), step_index, swap_together
    )
    return (input_grad[None], new_gain[None], new_gate[None], new_up[None], new_down[None])


def solution(mesh):
    in_specs = (
        P("rep", "fsdp", None),
        P("rep", "fsdp", None),
        P("rep", None),
        P("rep", None, "fsdp"),
        P("rep", None, "fsdp"),
        P("rep", "fsdp", None),
        P(),
    )
    out_specs = (
        P("rep", "fsdp", None),
        P("rep", None),
        P("rep", None, "fsdp"),
        P("rep", None, "fsdp"),
        P("rep", "fsdp", None),
    )
    return jax.shard_map(local, mesh=mesh, in_specs=in_specs, out_specs=out_specs, check_vma=False)
```

profile of v0, /device:TPU:16, one launch (start us, length us, event | category | flops | bytes accessed | tf_op | source)
XLA Modules:
  0.0 416.9 jit_solution(3565462379755001432)
XLA Ops:
  7.2 0.0 copy-start.5
  7.2 0.0 all-gather.4.cloned.1.call-start
  7.2 1.2 fusion.31
  8.4 1.8 fusion.28
  10.2 0.0 all-gather.4.cloned.1.call-update
  10.2 0.0 all-gather.6.cloned.1.call-start
  10.3 0.7 all-gather.6.cloned.1.call-update
  11.0 0.0 reduce-scatter.2.cloned.1.call-start
  11.0 1.6 copy.12
  12.6 0.0 copy-done.5
  12.6 0.3 copy.13
  12.9 0.0 copy-start
  13.0 0.1 bitcast_convert_fusion
  13.1 72.4 %all-gather.4.cloned.1.call-done = bf16[2048,2048]{1,0:T(8,128)(2,1)} async-done(((bf16[64,2048]{1,0:T(8,128)(2,1)}), bf16[2048,2048]{1,0:T(8,128)(2,1)}) %all-gather.4.cloned.1.call-update) | async-done | bytes 8388624 | tf_op jit(solution)/shard_map/all_gather | solution.py:54
  85.5 7.1 %convolution_multiply_fusion.1 = f32[2048,256]{0,1:T(8,128)} fusion(bf16[2048,2048]{1,0:T(8,128)(2,1)} %all-gather.4.cloned.1.call-done, bf16[2048,128]{0,1:T(8,128)(2,1)S(1)} %get-tuple-element.106, bf16[2048,128]{0,1:T(8,128)(2,1)S(1)} %get-tuple-element.107), kind=kOutput, calls=%fused_computation.6 | convolution fusion | flops 2150105088 | bytes 11534336 | tf_op jit(solution)/shard_map/dot_general | solution.py:55
  92.7 0.0 copy-done
  92.7 66.9 %all-gather.6.cloned.1.call-done = bf16[1,2048,2048]{2,1,0:T(8,128)(2,1)} async-done(((bf16[1,64,2048]{2,1,0:T(8,128)(2,1)}), bf16[1,2048,2048]{2,1,0:T(8,128)(2,1)}) %all-gather.6.cloned.1.call-update) | async-done | bytes 8388624 | tf_op jit(solution)/shard_map/all_gather | solution.py:61
  159.6 7.3 %multiply_convert_fusion.3 = (bf16[2048,128]{0,1:T(8,128)(2,1)S(1)}, bf16[2048,128]{0,1:T(8,128)(2,1)S(1)}) fusion(f32[2048,256]{0,1:T(8,128)} %convolution_multiply_fusion.1, bf16[1,2048,2048]{2,1,0:T(8,128)(2,1)} %all-gather.6.cloned.1.call-done, f32[1,128,2048]{2,1,0:T(8,128)} %param.15), kind=kOutput, calls=%fused_computation.28 | convolution fusion | flops 1077411840 | bytes 12582912 | tf_op jit(solution)/shard_map/dot_general | solution.py:70
  166.9 5.6 %multiply_convert_fusion = bf16[2048,2048]{1,0:T(8,128)(2,1)} fusion(bf16[2048,128]{0,1:T(8,128)(2,1)S(1)} %get-tuple-element.103, bf16[2048,128]{0,1:T(8,128)(2,1)S(1)} %get-tuple-element.102, bf16[2048,128]{0,1:T(8,128)(2,1)S(1)} %get-tuple-element.106, bf16[2048,128]{0,1:T(8,128)(2,1)S(1)} %get-tuple-element.107), kind=kOutput, calls=%fused_computation | convolution fusion | flops 2160066560 | bytes 10485760 | tf_op jit(solution)/shard_map/dot_general | solution.py:88
  172.5 0.0 reduce-scatter.2.cloned.1.call-update
  173.2 0.0 copy-start.1
  173.2 5.8 %convolution_multiply_fusion = f32[2048,256]{0,1:T(8,128)S(1)} fusion(bf16[2048,2048]{1,0:T(8,128)(2,1)} %all-gather.4.cloned.1.call-done, bf16[2048,128]{0,1:T(8,128)(2,1)S(1)} %get-tuple-element.103, bf16[2048,128]{0,1:T(8,128)(2,1)S(1)} %get-tuple-element.102), kind=kOutput, calls=%fused_computation.5 | convolution fusion | flops 2150105088 | bytes 11534336 | tf_op jit(solution)/shard_map/dot_general | solution.py:81
  179.1 0.0 copy-done.1
  179.1 0.0 copy-start.7
  179.1 0.0 copy-start.8
  179.1 0.3 fusion.13
  179.4 0.9 copy-done.7
  180.3 0.7 copy-done.8
  181.0 0.0 copy-start.2
  181.0 0.0 copy-start.6
  181.0 5.1 %fusion.10 = f32[128,2048]{1,0:T(8,128)S(1)} fusion(bf16[1,2048,2048]{2,1,0:T(8,128)(2,1)} %all-gather.6.cloned.1.call-done, f32[1,128,2048]{2,1,0:T(8,128)S(1)} %copy-done.7, f32[2048,256]{0,1:T(8,128)S(1)} %copy-done.8), kind=kOutput, calls=%fused_computation.9 | convolution fusion | flops 1075838976 | bytes 12582912 | tf_op jit(solution)/shard_map/dot_general | solution.py:63
  186.1 116.6 %reduce-scatter.2.cloned.1.call-done = bf16[64,2048]{1,0:T(8,128)(2,1)} async-done(((bf16[2048,2048]{1,0:T(8,128)(2,1)}), bf16[64,2048]{1,0:T(8,128)(2,1)}) %reduce-scatter.2.cloned.1.call-update) | async-done | bytes 262160 | tf_op jit(solution)/shard_map/reduce_scatter | solution.py:86
  302.7 0.0 copy-done.2
  302.7 0.0 copy-done.6
  302.7 1.3 fusion.30
  303.9 55.0 %psum.7 = f32[2048]{0:T(1024)S(1)} all-reduce(f32[2048]{0:T(1024)S(1)} %get-tuple-element.100), channel_id=1, replica_groups=mesh['rep'=8,'fsdp'=32] {'fsdp'}, use_global_device_ids=true, to_apply=%region_4.0 | all-reduce | flops 2048 | bytes 16384 | tf_op jit(solution)/shard_map/psum | solution.py:100
  359.0 40.3 %conditional.4 = (bf16[2048,128]{1,0:T(8,128)(2,1)}, bf16[2048,128]{1,0:T(8,128)(2,1)}, f32[2048]{0:T(1024)S(1)}, f32[128,2048]{1,0:T(8,128)}) conditional(s32[]{:T(128)} %clamp.3, (f32[2048]{0:T(1024)S(1)}, f32[2048,128]{0,1:T(8,128)S(1)}, f32[2048,128]{0,1:T(8,128)S(1)}, f32[128,2048]{1,0:T(8,128)S(1)}) %tuple.52, ...), branch_computations={%region_5.6_spmd, %region_6.7_spmd, %region_7.8_spmd} | conditional | flops 528384 | bytes 12624064
  359.2 1.0 copy.15
  360.2 0.5 collective-permute-start.1
  360.7 0.9 convert_element_type.109
  361.6 3.0 collective-permute-start.3
  364.5 1.0 copy.16
  365.5 0.5 collective-permute-start.2
  366.1 3.0 collective-permute-start
  369.1 28.1 %collective-permute-done = bf16[2048]{0:T(1024)(128)(2,1)S(1)} collective-permute-done((bf16[2048]{0:T(1024)(128)(2,1)S(1)}, bf16[2048]{0:T(1024)(128)(2,1)S(1)}, u32[]{:S(2)}, u32[]{:S(2)}) %collective-permute-start) | collective-permute-done | bytes 4128 | tf_op jit(solution)/shard_map/cond/branch_0_fun/ppermute | solution.py:15
  397.2 0.0 collective-permute-done.3
  397.2 2.1 convert_element_type.158
  399.3 0.0 collective-permute-done.1
  399.3 0.0 collective-permute-done.2
  399.3 0.6 add_multiply_fusion
  399.9 2.3 multiply_bitcast_fusion
  402.2 2.0 copy.22
  404.3 1.2 fusion.16
  405.4 1.3 copy.24
  406.7 1.2 copy.21
  408.0 0.0 copy-start.3
  408.0 0.0 copy-start.4
  408.0 0.1 fusion.18
  408.1 1.3 copy.23
  409.5 0.0 copy-done.3
  409.5 0.0 copy-done.4
  409.5 0.9 fusion.32
  (5 shorter events, 0.0 us)
Async XLA Ops:
  7.2 5.4 %copy-start.5 = (f32[1,2048,128]{2,1,0:T(8,128)S(1)}, f32[1,2048,128]{2,1,0:T(8,128)}, u32[]{:S(2)}) copy-start(f32[1,2048,128]{2,1,0:T(8,128)} %param.14) | copy-start | bytes 3145732
  7.2 78.4 %all-gather.4.cloned.1.call-start = ((), (), s32[]{:S(2)}) async-start(), calls=%async_computation.1 | async-start | bytes 8650752 | tf_op jit(solution)/shard_map/all_gather | solution.py:54
  10.2 149.4 %all-gather.6.cloned.1.call-start = ((), (), s32[]{:S(2)}) async-start(), calls=%async_computation.3 | async-start | bytes 8650752 | tf_op jit(solution)/shard_map/all_gather | solution.py:61
  11.0 291.7 %reduce-scatter.2.cloned.1.call-start = ((), (), s32[]{:S(2)}) async-start(), calls=%async_computation.2 | async-start | bytes 8650752 | tf_op jit(solution)/shard_map/reduce_scatter | solution.py:86
  12.9 79.7 %copy-start = (f32[1,2048,128]{1,2,0:T(8,128)}, f32[1,2048,128]{1,2,0:T(8,128)S(1)}, u32[]{:S(2)}) copy-start(f32[1,2048,128]{1,2,0:T(8,128)S(1)} %copy.13) | copy-start | bytes 3145732
  173.2 5.8 %copy-start.1 = (f32[1,2048,128]{1,2,0:T(8,128)S(1)}, f32[1,2048,128]{1,2,0:T(8,128)}, u32[]{:S(2)}) copy-start(f32[1,2048,128]{1,2,0:T(8,128)} %copy-done) | copy-start | bytes 3145732
  179.1 1.2 copy-start.7
  179.1 1.9 copy-start.8
  181.0 121.7 %copy-start.2 = (bf16[1,64,2048]{2,1,0:T(8,128)(2,1)S(1)}, bf16[1,64,2048]{2,1,0:T(8,128)(2,1)}, u32[]{:S(2)}) copy-start(bf16[1,64,2048]{2,1,0:T(8,128)(2,1)} %param.10) | copy-start | bytes 786436
  181.0 121.7 %copy-start.6 = (f32[1,2048]{1,0:T(1,128)S(1)}, f32[1,2048]{1,0:T(1,128)}, u32[]{:S(2)}) copy-start(f32[1,2048]{1,0:T(1,128)} %param.12) | copy-start | bytes 24580
  360.2 39.1 %collective-permute-start.1 = (bf16[2048,128]{1,0:T(8,128)(2,1)}, bf16[2048,128]{1,0:T(8,128)(2,1)}, u32[]{:S(2)}, u32[]{:S(2)}) collective-permute-start(bf16[2048,128]{1,0:T(8,128)(2,1)} %copy.15), channel_id=1, source_target_pairs={{0,32},{32,0},{64,96},{96,64},{128,160},{160,128},{192,224},{224,1... | collective-permute-start | bytes 1572872 | tf_op jit(solution)/shard_map/cond/branch_0_fun/ppermute | solution.py:15
  361.6 35.6 %collective-permute-start.3 = (bf16[128,2048]{1,0:T(8,128)(2,1)}, bf16[128,2048]{1,0:T(8,128)(2,1)}, u32[]{:S(2)}, u32[]{:S(2)}) collective-permute-start(bf16[128,2048]{1,0:T(8,128)(2,1)} %convert_element_type.109), channel_id=1, source_target_pairs={{0,32},{32,0},{64,96},{96,64},{128,160},{160,128},{192,224},{224,1... | collective-permute-start | bytes 1572872 | tf_op jit(solution)/shard_map/cond/branch_0_fun/ppermute | solution.py:15
  365.5 33.8 %collective-permute-start.2 = (bf16[2048,128]{1,0:T(8,128)(2,1)}, bf16[2048,128]{1,0:T(8,128)(2,1)}, u32[]{:S(2)}, u32[]{:S(2)}) collective-permute-start(bf16[2048,128]{1,0:T(8,128)(2,1)} %copy.16), channel_id=1, source_target_pairs={{0,32},{32,0},{64,96},{96,64},{128,160},{160,128},{192,224},{224,1... | collective-permute-start | bytes 1572872 | tf_op jit(solution)/shard_map/cond/branch_0_fun/ppermute | solution.py:15
  366.1 31.1 %collective-permute-start = (bf16[2048]{0:T(1024)(128)(2,1)S(1)}, bf16[2048]{0:T(1024)(128)(2,1)S(1)}, u32[]{:S(2)}, u32[]{:S(2)}) collective-permute-start(bf16[2048]{0:T(1024)(128)(2,1)S(1)} %convert_element_type.103), channel_id=1, source_target_pairs={{0,32},{32,0},{64,96},{96,64},{128,160},{160,128},{192,224},{224,1... | collective-permute-start | bytes 12296 | tf_op jit(solution)/shard_map/cond/branch_0_fun/ppermute | solution.py:15
  408.0 1.5 copy-start.3
  408.0 1.5 copy-start.4
Sparse Core Ops, SparseCore 0:
  10.4 75.0 all-gather.3
  87.4 72.1 all-gather.5
  172.7 129.9 reduce-scatter.1
where the time goes:
time: 418 us; the launch traced here: 417 us
  waiting for transfers between devices  285 us (68%)
  blocking collectives  55 us (13%)
  matrix products  31 us (7%)
  between operations  14.6 us (3%)
  other arithmetic  12.8 us (3%)
  local copies, waits for them, and re-layouts  11.4 us (3%)
  starting transfers between devices  7.18 us (2%)
    reduce_scatter x1, waiting for transfers between devices, local(): lax.psum_scatter((lax.dot_general(grad_both, both_weights, (((1,), (1,)),...  117 us
    all_gather x1, waiting for transfers between devices, local(): gathered = lax.all_gather(normed, 'fsdp', axis=0, tiled=True)  72.4 us
    all_gather x1, waiting for transfers between devices, local(): grad_all = lax.all_gather(cotangent[0], 'fsdp', axis=0, tiled=True)  66.9 us
    psum x1, blocking collectives, local(): grad_gain = lax.psum(jnp.sum(grad_normed * unit_rows, axis=0), 'fsdp')  55 us
    ppermute x4, waiting for transfers between devices, from_partner(): lax.ppermute(x, axis, [(i, i ^ 1 << distance) for i in range(lax.axis_siz...  28.1 us
    unnamed x24, local copies, waits for them, and re-layouts  9.41 us
  transfers between devices with their start and end apart: 7, of which 4 were waited for; matrix products, arithmetic and copies ran while one was open for 6% of the time, Pallas kernels for 0%

commit v1 on v0

v1 whole, which is shorter than its diff:
```python
import functools

import jax
import jax.numpy as jnp
from jax import lax
from jax.experimental import pallas as pl
from jax.experimental.pallas import tpu as pltpu
from jax.sharding import PartitionSpec as P

MESH = pl.DeviceIdType.MESH
F32 = jnp.float32
BF16 = jnp.bfloat16

learn_rate = 0.02
epsilon = 1e-05

NT = (((1,), (1,)), ((), ()))
NN = (((1,), (0,)), ((), ()))

OWN, FOUR = 6, 7
WIDTH = 512


def slot_of(direction, step):
    if step == 0:
        return OWN
    return 2 * (step - 1) + direction


def kernel(
    level,
    tok_hbm, cot_hbm, gain_hbm, wg_hbm, wu_hbm, wd_hbm,
    ig_out, gain_out, ng_out, nu_out, nd_out,
    tok, gain, raw, wt, wb, normed, cot, back, xt, terms,
    sib_out, sib_in, keep, y_out, y_in, x_out, x_in, rs_out, rs_in,
    gain_one, gain_two, gain_ring, gain_part, gain_new, ig,
    in_sem, out_sem, ag_s, ag_r, w_s, w_r, sib_s, sib_r, y_s, y_r, x_s, x_r,
    rs_s, rs_r, g_s, g_r,
):
    rep = lax.axis_index("rep")
    me = lax.axis_index("fsdp")
    n_fsdp = lax.axis_size("fsdp")
    width = tok.shape[1]
    rows = tok.shape[0]
    units = wt.shape[1]
    pieces = width // WIDTH
    count = 3 * pieces
    in_scale = width ** (-0.5)
    out_scale = (units * n_fsdp) ** (-0.5)

    up = (rep, lax.rem(me + 4, n_fsdp))
    down = (rep, lax.rem(me + n_fsdp - 4, n_fsdp))
    sib = (rep, me + 1 - 2 * lax.rem(me, 2))
    across = (rep, me + 2 - 4 * lax.rem(me // 2, 2))
    far = 1 << level
    partner = (rep + far - 2 * far * lax.rem(rep // far, 2), me)
    ring = (up, down)

    def remote(src, dst, send, recv, device):
        copy = pltpu.make_async_remote_copy(
            src_ref=src, dst_ref=dst, send_sem=send, recv_sem=recv,
            device_id=device, device_id_type=MESH,
        )
        copy.start()
        sent.append(copy)
        return copy

    sent = []

    loads = [
        pltpu.make_async_copy(cot_hbm, cot.at[OWN], in_sem.at[0]),
        pltpu.make_async_copy(tok_hbm, tok, in_sem.at[1]),
        pltpu.make_async_copy(gain_hbm, gain, in_sem.at[2]),
        pltpu.make_async_copy(wg_hbm, raw.at[0], in_sem.at[3]),
        pltpu.make_async_copy(wu_hbm, raw.at[1], in_sem.at[4]),
        pltpu.make_async_copy(wd_hbm, wt.at[2], in_sem.at[5]),
    ]
    for load in loads:
        load.start()

    barrier = pltpu.get_barrier_semaphore()
    for other in (up, down, sib, across, partner):
        pl.semaphore_signal(barrier, inc=1, device_id=other, device_id_type=MESH)
    pl.semaphore_wait(barrier, 5)

    def gather_step(which, buffer, step):
        copies = []
        for direction in (0, 1):
            src = buffer.at[slot_of(direction, step - 1)]
            if step < 4:
                dst = buffer.at[slot_of(direction, step)]
            else:
                half = pl.ds(direction * (rows // 2), rows // 2)
                src = src.at[half]
                dst = buffer.at[FOUR, half]
            copies.append(
                remote(src, dst, ag_s.at[which, direction, step - 1],
                       ag_r.at[which, direction, step - 1], ring[direction])
            )
        return copies

    loads[0].wait()
    cot_copies = gather_step(1, cot, 1)

    loads[1].wait()
    loads[2].wait()
    for r in range(0, rows, 16):
        part = pl.ds(r, 16)
        values = tok[part, :].astype(F32)
        inv_rms = lax.rsqrt(jnp.mean(values * values, axis=1, keepdims=True) + epsilon)
        normed[OWN, part, :] = ((values * inv_rms) * gain[...]).astype(BF16)
    normed_copies = gather_step(0, normed, 1)

    w_copies = []

    def share_weight(m):
        own = wb.at[m, pl.ds(0, units)]
        first = remote(own, wb.at[m, pl.ds(2 * units, units)], w_s.at[m, 0], w_r.at[m, 0], across)
        second = remote(own, wb.at[m, pl.ds(units, units)], w_s.at[m, 1], w_r.at[m, 1], sib)
        w_copies.append((first, second))

    for m in (0, 1):
        loads[3 + m].wait()
        for c in range(0, width, 128):
            turned = raw[m, c:c + 128, :].T
            wt[m, :, c:c + 128] = turned
            wb[m, 0:units, c:c + 128] = turned.astype(BF16)
        share_weight(m)
    loads[5].wait()
    wb[2, 0:units, :] = wt[2].astype(BF16)
    share_weight(2)

    def pass_weight(m):
        w_copies[m][0].wait_recv()
        src = wb.at[m, pl.ds(2 * units, units)]
        return remote(src, wb.at[m, pl.ds(3 * units, units)], w_s.at[m, 2], w_r.at[m, 2], sib)

    def forward(g, tile):
        n_rows = normed[2 * g:2 * g + 2].reshape(2 * rows, width)
        c_rows = cot[2 * g:2 * g + 2].reshape(2 * rows, width)
        cols = slice(tile * 2 * units, (tile + 1) * 2 * units)
        dot = functools.partial(lax.dot_general, dimension_numbers=NT, preferred_element_type=F32)
        gate_pre = dot(n_rows, wb[0, cols, :]) * in_scale
        up_pre = dot(n_rows, wb[1, cols, :]) * in_scale
        grad_hidden = dot(c_rows, wb[2, cols, :]) * out_scale
        sigmoid_gate = jax.nn.sigmoid(gate_pre)
        activated = gate_pre * sigmoid_gate
        hidden = activated * up_pre
        grad_gate = grad_hidden * up_pre * sigmoid_gate * (1.0 + gate_pre * (1.0 - sigmoid_gate))
        grad_up = grad_hidden * activated
        back[0, g, :, cols] = grad_gate.astype(BF16)
        back[1, g, :, cols] = grad_up.astype(BF16)
        lanes = slice(g * 2 * rows, (g + 1) * 2 * rows)
        xt[0, cols, lanes] = grad_gate.T.astype(BF16)
        xt[1, cols, lanes] = grad_up.T.astype(BF16)
        xt[2, cols, lanes] = hidden.T.astype(BF16)

    def term(g):
        for c in range(0, width, WIDTH):
            part = slice(c, c + WIDTH)
            value = lax.dot_general(back[0, g], wb[0, :, part], NN, preferred_element_type=F32)
            value += lax.dot_general(back[1, g], wb[1, :, part], NN, preferred_element_type=F32)
            value = (value * in_scale).astype(BF16)
            terms[2 * g:2 * g + 2, :, part] = value.reshape(2, rows, WIDTH)

    handed = []
    for step in (1, 2, 3):
        for copy in cot_copies:
            copy.wait_recv()
        cot_copies = gather_step(1, cot, step + 1)
        for copy in normed_copies:
            copy.wait_recv()
        normed_copies = gather_step(0, normed, step + 1)
        if step == 1:
            for m in range(3):
                w_copies[m][1].wait_recv()
        forward(step - 1, 0)
        handed.append(pass_weight(step - 1))
    for copy in handed:
        copy.wait_recv()
    for g in range(3):
        forward(g, 1)
    for g in range(3):
        term(g)
    for copy in cot_copies + normed_copies:
        copy.wait_recv()
    forward(3, 0)
    forward(3, 1)

    order = [(m, q) for m in (2, 0, 1) for q in range(pieces)]
    targets = (ng_out, nu_out, nd_out)
    sib_copies, y_copies, x_copies = [], [], []

    def product(i):
        m, q = order[i]
        cols = slice(q * WIDTH, (q + 1) * WIDTH)
        right = (cot if m == 2 else normed)[:, :, cols].reshape(8 * rows, WIDTH)
        scale = out_scale if m == 2 else in_scale
        for tile in (0, 1):
            part = slice(tile * 2 * units, (tile + 1) * 2 * units)
            value = lax.dot_general(xt[m, part, :], right, NN, preferred_element_type=F32) * scale
            keep[i, tile] = value[:units]
            sib_out[i, tile] = value[units:].astype(BF16)
        sib_copies.append(remote(sib_out.at[i], sib_in.at[i], sib_s.at[i], sib_r.at[i], sib))

    def add_sib(i):
        sib_copies[i].wait_recv()
        y_out[i] = (keep[i, 1] + sib_in[i, 1].astype(F32)).astype(BF16)
        y_copies.append(remote(y_out.at[i], y_in.at[i], y_s.at[i], y_r.at[i], across))
        keep[i, 0] += sib_in[i, 0].astype(F32)

    def add_across(i):
        m, q = order[i]
        y_copies[i].wait_recv()
        gradient = keep[i, 0] + y_in[i].astype(F32)
        new = wt[m, :, q * WIDTH:(q + 1) * WIDTH] - learn_rate * gradient
        keep[i, 0] = new
        x_out[i] = new.astype(BF16)
        x_copies.append(remote(x_out.at[i], x_in.at[i], x_s.at[i], x_r.at[i], partner))

    writes = []

    def average(i):
        m, q = order[i]
        x_copies[i].wait_recv()
        keep[i, 0] = 0.5 * (keep[i, 0] + x_in[i].astype(F32))
        write = pltpu.make_async_copy(
            keep.at[i, 0], targets[m].at[:, pl.ds(q * WIDTH, WIDTH)], out_sem.at[i]
        )
        write.start()
        writes.append(write)

    half = rows // 2
    rs_copies = {}

    def scatter_first():
        for direction in (0, 1):
            part = pl.ds(direction * half, half)
            rs_copies[direction] = remote(
                terms.at[FOUR, part], rs_in.at[direction, 0, part],
                rs_s.at[direction, 0], rs_r.at[direction, 0], ring[direction]
            )

    def scatter_step(step):
        for direction in (0, 1):
            rs_copies[direction].wait_recv()
            slot = slot_of(1 - direction, step)
            if step == 3:
                a = direction * half
                b = half - a
                mine = slice(a, a + half)
                rest = slice(b, b + half)
                rs_out[direction, 0, mine] = (
                    terms[slot, mine, :].astype(F32) + rs_in[direction, 0, mine, :].astype(F32)
                ).astype(BF16)
                rs_out[direction, 0, rest] = terms[slot, rest, :]
            else:
                rs_out[direction, 3 - step] = (
                    terms[slot].astype(F32) + rs_in[direction, 3 - step].astype(F32)
                ).astype(BF16)
            rs_copies[direction] = remote(
                rs_out.at[direction, 3 - step], rs_in.at[direction, 4 - step],
                rs_s.at[direction, 4 - step], rs_r.at[direction, 4 - step], ring[direction]
            )

    def scatter_last():
        for direction in (0, 1):
            rs_copies[direction].wait_recv()
        total = jnp.zeros((8, width), F32)
        for r in range(0, rows, 16):
            part = slice(r, r + 16)
            values = tok[part, :].astype(F32)
            inv_rms = lax.rsqrt(jnp.mean(values * values, axis=1, keepdims=True) + epsilon)
            unit = values * inv_rms
            grad = (
                terms[OWN, part, :].astype(F32)
                + rs_in[0, 3, part, :].astype(F32)
                + rs_in[1, 3, part, :].astype(F32)
            )
            product_ = grad * unit
            total += product_[:8] + product_[8:]
            scaled = grad * gain[...]
            mean = jnp.mean(scaled * unit, axis=1, keepdims=True)
            ig[part, :] = (
                cot[OWN, part, :].astype(F32) + inv_rms * (scaled - unit * mean)
            ).astype(BF16)
        gain_one[0] = total
        write = pltpu.make_async_copy(ig, ig_out, out_sem.at[count])
        write.start()
        writes.append(write)

    gain_copies = {}

    def gain_sib():
        gain_copies[0] = remote(gain_one.at[0], gain_one.at[1], g_s.at[0], g_r.at[0], sib)

    def gain_across():
        gain_copies[0].wait_recv()
        gain_two[0] = gain_one[0] + gain_one[1]
        gain_copies[1] = remote(gain_two.at[0], gain_two.at[1], g_s.at[1], g_r.at[1], across)

    def gain_ring_start():
        gain_copies[1].wait_recv()
        gain_ring[0] = gain_two[0] + gain_two[1]
        gain_copies["up"] = remote(gain_ring.at[0], gain_ring.at[1], g_s.at[2], g_r.at[2], up)
        gain_copies["down"] = remote(gain_ring.at[0], gain_ring.at[7], g_s.at[3], g_r.at[3], down)

    def gain_ring_step(step):
        gain_copies["up"].wait_recv()
        gain_copies["down"].wait_recv()
        gain_copies["up"] = remote(
            gain_ring.at[step - 1], gain_ring.at[step], g_s.at[2 * step], g_r.at[2 * step], up
        )
        if step < 4:
            gain_copies["down"] = remote(
                gain_ring.at[9 - step], gain_ring.at[8 - step],
                g_s.at[2 * step + 1], g_r.at[2 * step + 1], down
            )

    def gain_finish():
        gain_copies["up"].wait_recv()
        z = me // 4
        total = gain_ring[lax.rem(z + 8, 8)]
        for a in range(1, 8):
            total += gain_ring[lax.rem(z - a + 8, 8)]
        gradient = jnp.sum(total, axis=0, keepdims=True)
        gain_part[0] = jnp.broadcast_to(gain[...] - learn_rate * gradient, (8, width))
        gain_copies["x"] = remote(gain_part.at[0], gain_part.at[1], g_s.at[9], g_r.at[9], partner)

    def gain_average():
        gain_copies["x"].wait_recv()
        gain_new[...] = 0.5 * (gain_part[0, 0:1, :] + gain_part[1, 0:1, :])
        write = pltpu.make_async_copy(gain_new, gain_out, out_sem.at[count + 1])
        write.start()
        writes.append(write)

    product(0)
    product(1)
    add_sib(0)
    product(2)
    add_sib(1)
    term(3)
    scatter_first()
    for i in range(3, count):
        product(i)
        add_sib(i - 1)
        if i == 5:
            scatter_step(3)
    add_sib(count - 1)
    extra = {
        1: [lambda: scatter_step(2)],
        3: [lambda: scatter_step(1)],
        5: [scatter_last, gain_sib],
        6: [gain_across],
        7: [gain_ring_start],
        8: [lambda: gain_ring_step(2)],
        9: [lambda: gain_ring_step(3)],
        10: [lambda: gain_ring_step(4)],
        11: [gain_finish],
    }
    for i in range(count):
        add_across(i)
        for action in extra.get(i, ()):
            action()
        if i >= 3:
            average(i - 3)
    for i in range(count - 3, count):
        average(i)
    gain_average()

    for copy in sent:
        copy.wait_send()
    for write in writes:
        write.wait()


def step_on_device(level, tokens, cotangent, gain, w_gate, w_up, w_down):
    rows, width = tokens.shape
    units = w_down.shape[0]
    count = 3 * (width // WIDTH)
    anywhere = pl.BlockSpec(memory_space=pl.ANY)
    dma = pltpu.SemaphoreType.DMA
    return pl.pallas_call(
        functools.partial(kernel, level),
        out_shape=(
            jax.ShapeDtypeStruct((rows, width), BF16),
            jax.ShapeDtypeStruct((1, width), F32),
            jax.ShapeDtypeStruct((units, width), F32),
            jax.ShapeDtypeStruct((units, width), F32),
            jax.ShapeDtypeStruct((units, width), F32),
        ),
        in_specs=[anywhere] * 6,
        out_specs=(anywhere,) * 5,
        scratch_shapes=[
            pltpu.VMEM((rows, width), BF16),
            pltpu.VMEM((1, width), F32),
            pltpu.VMEM((2, width, units), F32),
            pltpu.VMEM((3, units, width), F32),
            pltpu.VMEM((3, 4 * units, width), BF16),
            pltpu.VMEM((8, rows, width), BF16),
            pltpu.VMEM((8, rows, width), BF16),
            pltpu.VMEM((2, 4, 2 * rows, 4 * units), BF16),
            pltpu.VMEM((3, 4 * units, 8 * rows), BF16),
            pltpu.VMEM((8, rows, width), BF16),
            pltpu.VMEM((count, 2, units, WIDTH), BF16),
            pltpu.VMEM((count, 2, units, WIDTH), BF16),
            pltpu.VMEM((count, 2, units, WIDTH), F32),
            pltpu.VMEM((count, units, WIDTH), BF16),
            pltpu.VMEM((count, units, WIDTH), BF16),
            pltpu.VMEM((count, units, WIDTH), BF16),
            pltpu.VMEM((count, units, WIDTH), BF16),
            pltpu.VMEM((2, 3, rows, width), BF16),
            pltpu.VMEM((2, 4, rows, width), BF16),
            pltpu.VMEM((2, 8, width), F32),
            pltpu.VMEM((2, 8, width), F32),
            pltpu.VMEM((8, 8, width), F32),
            pltpu.VMEM((2, 8, width), F32),
            pltpu.VMEM((1, width), F32),
            pltpu.VMEM((rows, width), BF16),
            dma((6,)),
            dma((count + 2,)),
            dma((2, 2, 4)),
            dma((2, 2, 4)),
            dma((3, 3)),
            dma((3, 3)),
            dma((count,)),
            dma((count,)),
            dma((count,)),
            dma((count,)),
            dma((count,)),
            dma((count,)),
            dma((2, 4)),
            dma((2, 4)),
            dma((10,)),
            dma((10,)),
        ],
        compiler_params=pltpu.CompilerParams(
            collective_id=level, has_side_effects=True, vmem_limit_bytes=60 * 2**20
        ),
        cost_estimate=pl.CostEstimate(
            flops=8 * 2**30, bytes_accessed=8 * 2**20, transcendentals=2**18
        ),
    )(tokens, cotangent, gain, w_gate, w_up, w_down)


def local(tokens, cotangent, gain, w_gate, w_up, w_down, step_index):
    level_count = lax.axis_size("rep").bit_length() - 1
    branches = [functools.partial(step_on_device, level) for level in range(level_count)]
    input_grad, new_gain, gate_t, up_t, new_down = lax.switch(
        step_index[0] % level_count, branches,
        tokens[0], cotangent[0], gain, w_gate[0], w_up[0], w_down[0],
    )
    return (input_grad[None], new_gain, gate_t.T[None], up_t.T[None], new_down[None])


def solution(mesh):
    in_specs = (
        P("rep", "fsdp", None),
        P("rep", "fsdp", None),
        P("rep", None),
        P("rep", None, "fsdp"),
        P("rep", None, "fsdp"),
        P("rep", "fsdp", None),
        P(),
    )
    out_specs = (
        P("rep", "fsdp", None),
        P("rep", None),
        P("rep", None, "fsdp"),
        P("rep", None, "fsdp"),
        P("rep", "fsdp", None),
    )
    return jax.shard_map(local, mesh=mesh, in_specs=in_specs, out_specs=out_specs, check_vma=False)
```

time: 418 us -> 143 us (0.34)
  waiting for transfers between devices: 285 us -> 0 us
  Pallas kernels: 0 us -> 133 us
  blocking collectives: 55 us -> 0 us
  matrix products: 31 us -> 0 us
  between operations: 14.6 us -> 1.31 us
  other arithmetic: 12.8 us -> 0 us
  starting transfers between devices: 7.18 us -> 0 us
  local copies, waits for them, and re-layouts: 11.4 us -> 5.57 us
    all_gather x2 -> x0, waiting for transfers between devices: 139 us -> none  [the longest x1 72.4 us: local(): gathered = lax.all_gather(normed, 'fsdp', axis=0, tiled=True)]
    pallas_call x0 -> x1, Pallas kernels: none -> 133 us  [step_on_device(): pl.pallas_call(functools.partial(kernel, level), out_shape=(jax.ShapeDtyp...]
    reduce_scatter x1 -> x0, waiting for transfers between devices: 117 us -> none  [local(): lax.psum_scatter((lax.dot_general(grad_both, both_weights, (((1,), (1,)),...]
    psum x1 -> x0, blocking collectives: 55 us -> none  [local(): grad_gain = lax.psum(jnp.sum(grad_normed * unit_rows, axis=0), 'fsdp')]
    dot_general x5 -> x0, matrix products: 31 us -> none  [the longest x1 7.29 us: local(): lax.dot_general(grad_all, down_b, (((1,), (1,)), ((), ())), preferred_ele...]
    ppermute x4 -> x0, waiting for transfers between devices: 28.1 us -> none  [from_partner(): lax.ppermute(x, axis, [(i, i ^ 1 << distance) for i in range(lax.axis_siz...]
    ppermute x4 -> x0, starting transfers between devices: 7.06 us -> none  [from_partner(): lax.ppermute(x, axis, [(i, i ^ 1 << distance) for i in range(lax.axis_siz...]
    unnamed x24 -> x5, local copies, waits for them, and re-layouts: 9.41 us -> 2.95 us
  transfers between devices with their start and end apart: 7 -> 0, of which waited for: 4 -> 0; matrix products, arithmetic and copies ran while one was open for 6% -> 0% of each run, Pallas kernels for 0% -> 0%
where the time goes in v1:
time: 143 us; the launch traced here: 141 us
  Pallas kernels  133 us (93%)
  local copies, waits for them, and re-layouts  5.57 us (4%)
    pallas_call x1, Pallas kernels, step_on_device(): pl.pallas_call(functools.partial(kernel, level), out_shape=(jax.ShapeDtyp...  133 us
    unnamed x5, local copies, waits for them, and re-layouts  2.95 us

profile of v1, /device:TPU:16, one launch (start us, length us, event | category | flops | bytes accessed | tf_op | source)
XLA Modules:
  0.0 140.7 jit_solution(12193371002315534162)
XLA Ops:
  1.3 0.0 copy-start
  1.3 0.7 copy-done
  2.0 133.9 %conditional.1 = ((bf16[64,2048]{1,0:T(8,128)(2,1)S(1)}, f32[1,2048]{1,0:T(1,128)S(1)}, f32[128,2048]{1,0:T(8,128)S(1)}, f32[128,2048]{1,0:T(8,128)S(1)}, f32[128,2048]{1,0:T(8,128)S(1)})) conditional(s32[]{:T(128)} %clamp.3, (bf16[64,2048]{1,0:T(8,128)(2,1)}, bf16[64,2048]{1,0:T(8,128)(2,1)}, f32[1,2048]{1,0:T(1,128)S(1)}, ...), branch_computations={%region_0.1_spmd, %region_1.2_spmd, %region_2.3_spmd} | conditional | flops 8589934592 | bytes 8388616 | solution.py:449
  2.0 133.3 %branch_0_fun.1 = (bf16[64,2048]{1,0:T(8,128)(2,1)S(1)}, f32[1,2048]{1,0:T(1,128)S(1)}, f32[128,2048]{1,0:T(8,128)S(1)}, f32[128,2048]{1,0:T(8,128)S(1)}, f32[128,2048]{1,0:T(8,128)S(1)}) custom-call(bf16[64,2048]{1,0:T(8,128)(2,1)} %get-tuple-element.59.tok_hbm, bf16[64,2048]{1,0:T(8,128)(2,1)} %get-tuple-element.60.cot_hbm, ...), custom_call_target="tpu_custom_call" | custom-call | flops 8589934592 | bytes 8388608 | tf_op jit(solution)/shard_map/cond/branch_0_fun/pallas_call | solution.py:383
  135.9 1.3 copy.13
  137.2 1.3 copy.12
  138.5 0.7 copy.33
  139.2 0.6 copy.34
  139.8 1.0 copy.35
Async XLA Ops:
  1.3 0.7 copy-start

commit v2 on v1

v2 whole, which is shorter than its diff:
```python
import functools

import jax
import jax.numpy as jnp
from jax import lax
from jax.experimental import pallas as pl
from jax.experimental.pallas import tpu as pltpu
from jax.sharding import PartitionSpec as P

MESH = pl.DeviceIdType.MESH
F32 = jnp.float32
BF16 = jnp.bfloat16

learn_rate = 0.02
epsilon = 1e-05

NT = (((1,), (1,)), ((), ()))
NN = (((1,), (0,)), ((), ()))

OWN, FOUR = 6, 7
DEPTH = 3
WIDTH = 512


def kernel(
    level,
    tok_hbm, cot_hbm, gain_hbm, wg_hbm, wu_hbm, wd_hbm,
    ig_out, gain_out, ng_out, nu_out, nd_out,
    tok, gain, raw, wt, wb, normed, cot, back, xt, terms,
    sib_out, sib_in, keep, y_out, y_in, x_out, x_in, rs_out, rs_in, slopes, turned,
    gain_one, gain_two, gain_ring, gain_part, gain_new, ig,
    in_sem, out_sem, ag_s, ag_r, w_s, w_r, sib_s, sib_r, y_s, y_r, x_s, x_r,
    rs_s, rs_r, g_s, g_r,
):
    rep = lax.axis_index("rep")
    me = lax.axis_index("fsdp")
    n_fsdp = lax.axis_size("fsdp")
    width = tok.shape[1]
    rows = tok.shape[0]
    units = wt.shape[1]
    pieces = width // WIDTH
    count = 3 * pieces
    in_scale = width ** (-0.5)
    out_scale = (units * n_fsdp) ** (-0.5)

    up = (rep, lax.rem(me + 4, n_fsdp))
    down = (rep, lax.rem(me + n_fsdp - 4, n_fsdp))
    sib = (rep, me + 1 - 2 * lax.rem(me, 2))
    across = (rep, me + 2 - 4 * lax.rem(me // 2, 2))
    far = 1 << level
    partner = (rep + far - 2 * far * lax.rem(rep // far, 2), me)
    ring = (up, down)

    def remote(src, dst, send, recv, device):
        return pltpu.make_async_remote_copy(
            src_ref=src, dst_ref=dst, send_sem=send, recv_sem=recv,
            device_id=device, device_id_type=MESH,
        )

    def at_tile(start, size):
        return pl.ds(pl.multiple_of(start, size), size)

    loads = [
        pltpu.make_async_copy(cot_hbm, cot.at[OWN], in_sem.at[0]),
        pltpu.make_async_copy(tok_hbm, tok, in_sem.at[1]),
        pltpu.make_async_copy(gain_hbm, gain, in_sem.at[2]),
        pltpu.make_async_copy(wg_hbm, raw.at[0], in_sem.at[3]),
        pltpu.make_async_copy(wu_hbm, raw.at[1], in_sem.at[4]),
        pltpu.make_async_copy(wd_hbm, wt.at[2], in_sem.at[5]),
    ]
    for load in loads:
        load.start()

    barrier = pltpu.get_barrier_semaphore()
    for other in (up, down, sib, across, partner):
        pl.semaphore_signal(barrier, inc=1, device_id=other, device_id_type=MESH)
    pl.semaphore_wait(barrier, 5)

    def gather(which, direction, step):
        buffer = (normed, cot)[which]
        first = 1 // step
        src = buffer.at[first * OWN + (1 - first) * (2 * (step - 2) + direction)]
        return remote(
            src, buffer.at[2 * (step - 1) + direction],
            ag_s.at[which, direction, step - 1], ag_r.at[which, direction, step - 1],
            ring[direction],
        )

    def gather_half(which, direction):
        buffer = (normed, cot)[which]
        part = pl.ds(direction * half, half)
        return remote(
            buffer.at[4 + direction, part], buffer.at[FOUR, part],
            ag_s.at[which, direction, 3], ag_r.at[which, direction, 3], ring[direction],
        )

    half = rows // 2
    loads[1].wait()
    loads[2].wait()

    @pl.loop(0, rows // 16)
    def _(r):
        part = at_tile(r * 16, 16)
        values = tok[part, :].astype(F32)
        inv_rms = lax.rsqrt(jnp.mean(values * values, axis=1, keepdims=True) + epsilon)
        normed[OWN, part, :] = ((values * inv_rms) * gain[...]).astype(BF16)

    for direction in (0, 1):
        gather(0, direction, 1).start()
    loads[0].wait()
    for direction in (0, 1):
        gather(1, direction, 1).start()

    def weight_across(m):
        return remote(
            wb.at[m, pl.ds(0, units)], wb.at[m, pl.ds(2 * units, units)],
            w_s.at[m, 0], w_r.at[m, 0], across,
        )

    def weight_sib(m):
        return remote(
            wb.at[m, pl.ds(0, units)], wb.at[m, pl.ds(units, units)],
            w_s.at[m, 1], w_r.at[m, 1], sib,
        )

    def weight_passed(m):
        return remote(
            wb.at[m, pl.ds(2 * units, units)], wb.at[m, pl.ds(3 * units, units)],
            w_s.at[m, 2], w_r.at[m, 2], sib,
        )

    for m in (0, 1):
        loads[3 + m].wait()

        @pl.loop(0, width // 128)
        def _(c):
            cols = at_tile(c * 128, 128)
            block = raw[m, cols, :].T
            wt[m, :, cols] = block
            wb[m, 0:units, cols] = block.astype(BF16)

        weight_across(m).start()
        weight_sib(m).start()
    loads[5].wait()

    @pl.loop(0, width // 128)
    def _(c):
        cols = at_tile(c * 128, 128)
        wb[2, 0:units, cols] = wt[2, :, cols].astype(BF16)

    weight_across(2).start()
    weight_sib(2).start()

    def tokens_of(buffer, g):
        return buffer[pl.ds(2 * g, 2)].reshape(2 * rows, width)

    def lanes_of(g):
        return at_tile(g * (2 * rows), 2 * rows)

    dot_nt = functools.partial(lax.dot_general, dimension_numbers=NT, preferred_element_type=F32)

    def forward(g, tile):
        cols = at_tile(tile * (2 * units), 2 * units)
        group = tokens_of(normed, g)
        gate_pre = dot_nt(group, wb[0, cols, :]) * in_scale
        up_pre = dot_nt(group, wb[1, cols, :]) * in_scale
        sigmoid_gate = jax.nn.sigmoid(gate_pre)
        activated = gate_pre * sigmoid_gate
        xt[2, cols, lanes_of(g)] = (activated * up_pre).T.astype(BF16)
        slopes[0, g, :, cols] = up_pre * sigmoid_gate * (1.0 + gate_pre * (1.0 - sigmoid_gate))
        slopes[1, g, :, cols] = activated

    def backward(g, tile):
        cols = at_tile(tile * (2 * units), 2 * units)
        grad_hidden = dot_nt(tokens_of(cot, g), wb[2, cols, :]) * out_scale
        for n in (0, 1):
            grad = grad_hidden * slopes[n, g, :, cols]
            back[n, g, :, cols] = grad.astype(BF16)
            xt[n, cols, lanes_of(g)] = grad.T.astype(BF16)

    def term(g):
        @pl.loop(0, pieces)
        def _(c):
            part = at_tile(c * WIDTH, WIDTH)
            value = lax.dot_general(back[0, g], wb[0, :, part], NN, preferred_element_type=F32)
            value += lax.dot_general(back[1, g], wb[1, :, part], NN, preferred_element_type=F32)
            value = value * in_scale
            terms[pl.ds(2 * g, 2), :, part] = value.astype(BF16).reshape(2, rows, WIDTH)
            along = value * normed[pl.ds(2 * g, 2), :, part].reshape(2 * rows, WIDTH).astype(F32)
            gain_one[0, :, part] += jnp.sum(along.reshape(rows // 4, 8, WIDTH), axis=0)

    gain_one[0] = jnp.zeros((8, width), F32)

    @pl.loop(0, 4)
    def _(i):
        step = i + 1

        @pl.when(i < 3)
        def _():
            for direction in (0, 1):
                gather(0, direction, step).wait_recv()

        @pl.when(i < 2)
        def _():
            for direction in (0, 1):
                gather(0, direction, step + 1).start()

        @pl.when(i == 2)
        def _():
            for direction in (0, 1):
                gather_half(0, direction).start()

        @pl.when(i == 3)
        def _():
            for direction in (0, 1):
                gather_half(0, direction).wait_recv()

        @pl.when(i == 0)
        def _():
            for m in range(3):
                weight_sib(m).wait_recv()

        forward(i, 0)

        @pl.when(i < 3)
        def _():
            for direction in (0, 1):
                gather(1, direction, step).wait_recv()

        @pl.when(i < 2)
        def _():
            for direction in (0, 1):
                gather(1, direction, step + 1).start()

        @pl.when(i == 2)
        def _():
            for direction in (0, 1):
                gather_half(1, direction).start()

        @pl.when(i < 3)
        def _():
            weight_across(i).wait_recv()
            weight_passed(i).start()
            backward(i, 0)

        @pl.when(i == 1)
        def _():
            for m in (0, 1):
                weight_passed(m).wait_recv()

        low = i - i * (1 - i // 2)
        high = i + 1 - 1 // (i + 1)

        @pl.loop(low, high)
        def _(g):
            forward(g, 1)

    for direction in (0, 1):
        gather_half(1, direction).wait_recv()

    def scatter_first(direction):
        part = pl.ds(direction * half, half)
        return remote(
            terms.at[FOUR, part], rs_in.at[direction, 0, part],
            rs_s.at[direction, 0], rs_r.at[direction, 0], ring[direction],
        )

    def scatter_send(direction, step):
        return remote(
            rs_out.at[direction, 3 - step], rs_in.at[direction, 4 - step],
            rs_s.at[direction, 4 - step], rs_r.at[direction, 4 - step], ring[direction],
        )

    def scatter_step(step):
        for direction in (0, 1):
            if step == 3:
                scatter_first(direction).wait_recv()
            else:
                scatter_send(direction, step + 1).wait_recv()
            slot = 2 * (step - 1) + 1 - direction

            @pl.loop(0, rows // 16)
            def _(r):
                part = at_tile(r * 16, 16)
                value = terms[slot, part, :].astype(F32)
                if step == 3:
                    inside = (r // (half // 16)) == direction
                    came = jnp.where(inside, rs_in[direction, 0, part, :].astype(F32), 0.0)
                else:
                    came = rs_in[direction, 3 - step, part, :].astype(F32)
                rs_out[direction, 3 - step, part, :] = (value + came).astype(BF16)

            scatter_send(direction, step).start()

    def scatter_last():
        for direction in (0, 1):
            scatter_send(direction, 1).wait_recv()
        @pl.loop(0, rows // 16)
        def _(r):
            part = at_tile(r * 16, 16)
            values = tok[part, :].astype(F32)
            inv_rms = lax.rsqrt(jnp.mean(values * values, axis=1, keepdims=True) + epsilon)
            unit = values * inv_rms
            grad = (
                terms[OWN, part, :].astype(F32)
                + rs_in[0, 3, part, :].astype(F32)
                + rs_in[1, 3, part, :].astype(F32)
            )
            scaled = grad * gain[...]
            mean = jnp.mean(scaled * unit, axis=1, keepdims=True)
            ig[part, :] = (
                cot[OWN, part, :].astype(F32) + inv_rms * (scaled - unit * mean)
            ).astype(BF16)

        ig_write().start()

    def ig_write():
        return pltpu.make_async_copy(ig, ig_out, out_sem.at[count])

    def gain_copy(name, step=1):
        if name == "sib":
            src, dst, sem, device = gain_one.at[0], gain_one.at[1], 0, sib
        elif name == "across":
            src, dst, sem, device = gain_two.at[0], gain_two.at[1], 1, across
        elif name == "partner":
            src, dst, sem, device = gain_part.at[0], gain_part.at[1], 9, partner
        elif name == "up":
            src, dst, sem, device = gain_ring.at[step - 1], gain_ring.at[step], 2 * step, up
        else:
            src, dst, sem, device = (
                gain_ring.at[(9 - step) % 8], gain_ring.at[8 - step], 2 * step + 1, down
            )
        return remote(src, dst, g_s.at[sem], g_r.at[sem], device)

    def gain_sib():
        gain_copy("sib").start()

    def gain_across():
        gain_copy("sib").wait_recv()
        gain_two[0] = gain_one[0] + gain_one[1]
        gain_copy("across").start()

    def gain_ring_start():
        gain_copy("across").wait_recv()
        gain_ring[0] = gain_two[0] + gain_two[1]
        gain_copy("up").start()
        gain_copy("down").start()

    def gain_ring_step(step):
        gain_copy("up", step - 1).wait_recv()
        gain_copy("down", step - 1).wait_recv()
        gain_copy("up", step).start()
        if step < 4:
            gain_copy("down", step).start()

    def gain_finish():
        gain_copy("up", 4).wait_recv()
        z = me // 4
        total = gain_ring[lax.rem(z + 8, 8)]
        for a in range(1, 8):
            total += gain_ring[lax.rem(z - a + 8, 8)]
        gradient = jnp.sum(total, axis=0, keepdims=True) / gain[...]
        gain_part[0] = jnp.broadcast_to(gain[...] - learn_rate * gradient, (8, width))
        gain_copy("partner").start()

    def gain_write():
        return pltpu.make_async_copy(gain_new, gain_out, out_sem.at[count + 1])

    def gain_average():
        gain_copy("partner").wait_recv()
        gain_new[...] = 0.5 * (gain_part[0, 0:1, :] + gain_part[1, 0:1, :])
        gain_write().start()

    def piece(i):
        block = i // pieces
        m = block + 2 - 3 * ((block + 2) // 3)
        return m, at_tile((i - block * pieces) * WIDTH, WIDTH)

    def sib_copy(i):
        return remote(sib_out.at[i], sib_in.at[i], sib_s.at[i], sib_r.at[i], sib)

    def y_copy(i):
        return remote(y_out.at[i], y_in.at[i], y_s.at[i], y_r.at[i], across)

    def x_copy(i):
        return remote(x_out.at[i], x_in.at[i], x_s.at[i], x_r.at[i], partner)

    def product(i, m, buffer, scale):
        _m, cols = piece(i)
        right = buffer[:, :, cols].reshape(8 * rows, WIDTH)
        for tile in (0, 1):
            part = slice(tile * 2 * units, (tile + 1) * 2 * units)
            value = lax.dot_general(xt[m, part, :], right, NN, preferred_element_type=F32)
            value = value * scale
            keep[i, tile] = value[:units]
            sib_out[i, tile] = value[units:].astype(BF16)
        sib_copy(i).start()

    def add_sib(i):
        sib_copy(i).wait_recv()
        y_out[i] = (keep[i, 1] + sib_in[i, 1].astype(F32)).astype(BF16)
        keep[i, 0] += sib_in[i, 0].astype(F32)

    def add_across(i):
        m, cols = piece(i)
        y_copy(i).wait_recv()
        new = wt[m, :, cols] - learn_rate * (keep[i, 0] + y_in[i].astype(F32))
        keep[i, 0] = new
        x_out[i] = new.astype(BF16)
        x_copy(i).start()

        @pl.when(i < count - DEPTH)
        def _():
            y_copy(i + DEPTH).start()

    def write(target, i):
        m, cols = piece(i)
        return pltpu.make_async_copy(keep.at[i, 0], target.at[:, cols], out_sem.at[i])

    def write_turned(target, i):
        m, cols = piece(i)
        return pltpu.make_async_copy(turned.at[i], target.at[cols], out_sem.at[i])

    def average(i):
        x_copy(i).wait_recv()
        keep[i, 0] = 0.5 * (keep[i, 0] + x_in[i].astype(F32))

        @pl.when(i < pieces)
        def _():
            write(nd_out, i).start()

        @pl.when(i >= pieces)
        def _():
            turned[i] = keep[i, 0].T

        @pl.when((i >= pieces) & (i < 2 * pieces))
        def _():
            write_turned(ng_out, i).start()

        @pl.when(i >= 2 * pieces)
        def _():
            write_turned(nu_out, i).start()

    @pl.loop(0, pieces)
    def _(i):
        product(i, 2, cot, out_scale)

    weight_passed(2).wait_recv()

    @pl.loop(0, 5)
    def _(j):
        last = 2 // (j + 1) - 1 // (j + 1)
        backward(3 * last + (j - 2) * (1 - last), 1 - 1 // (j + 1))

        @pl.when(j < pieces)
        def _():
            add_sib(j)

        @pl.when(j < DEPTH)
        def _():
            y_copy(j).start()

        @pl.when(j == 1)
        def _():
            term(3)
            for direction in (0, 1):
                scatter_first(direction).start()

    @pl.loop(pieces, count)
    def _(i):
        m, _cols = piece(i)
        product(i, m, normed, in_scale)

        @pl.when(i > pieces)
        def _():
            add_sib(i - 1)

        @pl.when(i < pieces + 3)
        def _():
            term(2 + pieces - i)

        @pl.when(i == pieces + 3)
        def _():
            scatter_step(3)
            gain_sib()

        for p, at in enumerate((pieces + 2, pieces + 5)):
            @pl.when(i == at)
            def _():
                add_across(p)

    add_sib(count - 1)

    extra = {
        2: gain_across,
        3: gain_ring_start,
        4: lambda: (scatter_step(2), gain_ring_step(2)),
        5: lambda: gain_ring_step(3),
        6: lambda: gain_ring_step(4),
        7: lambda: (scatter_step(1), gain_finish()),
        10: scatter_last,
    }

    @pl.loop(2, count + 2)
    def _(i):
        @pl.when(i < count)
        def _():
            add_across(i)

        for at, action in extra.items():
            @pl.when(i == at)
            def _():
                action()

        average(i - 2)

    gain_average()

    for which in (0, 1):
        for direction in (0, 1):
            for step in (1, 2, 3):
                gather(which, direction, step).wait_send()
            gather_half(which, direction).wait_send()
    for m in range(3):
        for copy in (weight_across, weight_sib, weight_passed):
            copy(m).wait_send()
    for direction in (0, 1):
        scatter_first(direction).wait_send()
        for step in (3, 2, 1):
            scatter_send(direction, step).wait_send()
    for name in ("sib", "across", "partner"):
        gain_copy(name).wait_send()
    for step in (1, 2, 3, 4):
        gain_copy("up", step).wait_send()
        if step < 4:
            gain_copy("down", step).wait_send()

    @pl.loop(0, count)
    def _(i):
        sib_copy(i).wait_send()
        y_copy(i).wait_send()
        x_copy(i).wait_send()
        write(nd_out, i).wait()

    ig_write().wait()
    gain_write().wait()


def step_on_device(level, tokens, cotangent, gain, w_gate, w_up, w_down):
    rows, width = tokens.shape
    units = w_down.shape[0]
    count = 3 * (width // WIDTH)
    anywhere = pl.BlockSpec(memory_space=pl.ANY)
    dma = pltpu.SemaphoreType.DMA
    return pl.pallas_call(
        functools.partial(kernel, level),
        out_shape=(
            jax.ShapeDtypeStruct((rows, width), BF16),
            jax.ShapeDtypeStruct((1, width), F32),
            jax.ShapeDtypeStruct((width, units), F32),
            jax.ShapeDtypeStruct((width, units), F32),
            jax.ShapeDtypeStruct((units, width), F32),
        ),
        in_specs=[anywhere] * 6,
        out_specs=(anywhere,) * 5,
        scratch_shapes=[
            pltpu.VMEM((rows, width), BF16),
            pltpu.VMEM((1, width), F32),
            pltpu.VMEM((2, width, units), F32),
            pltpu.VMEM((3, units, width), F32),
            pltpu.VMEM((3, 4 * units, width), BF16),
            pltpu.VMEM((8, rows, width), BF16),
            pltpu.VMEM((8, rows, width), BF16),
            pltpu.VMEM((2, 4, 2 * rows, 4 * units), BF16),
            pltpu.VMEM((3, 4 * units, 8 * rows), BF16),
            pltpu.VMEM((8, rows, width), BF16),
            pltpu.VMEM((count, 2, units, WIDTH), BF16),
            pltpu.VMEM((count, 2, units, WIDTH), BF16),
            pltpu.VMEM((count, 2, units, WIDTH), F32),
            pltpu.VMEM((count, units, WIDTH), BF16),
            pltpu.VMEM((count, units, WIDTH), BF16),
            pltpu.VMEM((count, units, WIDTH), BF16),
            pltpu.VMEM((count, units, WIDTH), BF16),
            pltpu.VMEM((2, 3, rows, width), BF16),
            pltpu.VMEM((2, 4, rows, width), BF16),
            pltpu.VMEM((2, 4, 2 * rows, 4 * units), F32),
            pltpu.VMEM((count, WIDTH, units), F32),
            pltpu.VMEM((2, 8, width), F32),
            pltpu.VMEM((2, 8, width), F32),
            pltpu.VMEM((8, 8, width), F32),
            pltpu.VMEM((2, 8, width), F32),
            pltpu.VMEM((1, width), F32),
            pltpu.VMEM((rows, width), BF16),
            dma((6,)),
            dma((count + 2,)),
            dma((2, 2, 4)),
            dma((2, 2, 4)),
            dma((3, 3)),
            dma((3, 3)),
            dma((count,)),
            dma((count,)),
            dma((count,)),
            dma((count,)),
            dma((count,)),
            dma((count,)),
            dma((2, 4)),
            dma((2, 4)),
            dma((10,)),
            dma((10,)),
        ],
        compiler_params=pltpu.CompilerParams(
            collective_id=level, has_side_effects=True, vmem_limit_bytes=60 * 2**20
        ),
        cost_estimate=pl.CostEstimate(
            flops=8 * 2**30, bytes_accessed=8 * 2**20, transcendentals=2**18
        ),
    )(tokens, cotangent, gain, w_gate, w_up, w_down)


def local(tokens, cotangent, gain, w_gate, w_up, w_down, step_index):
    level_count = lax.axis_size("rep").bit_length() - 1
    branches = [functools.partial(step_on_device, level) for level in range(level_count)]
    input_grad, new_gain, new_gate, new_up, new_down = lax.switch(
        step_index[0] % level_count, branches,
        tokens[0], cotangent[0], gain, w_gate[0], w_up[0], w_down[0],
    )
    results = place_results(
        input_grad[None], new_gain, new_gate[None], new_up[None], new_down[None]
    )
    return tuple(results)


def place_results(*arrays):
    def body(*refs):
        n = len(refs) // 2
        sems = refs[-1]
        copies = [pltpu.make_async_copy(refs[i], refs[n + i], sems.at[i]) for i in range(n)]
        for copy in copies:
            copy.start()
        for copy in copies:
            copy.wait()

    anywhere = pl.BlockSpec(memory_space=pl.ANY)
    return pl.pallas_call(
        body,
        out_shape=tuple(jax.ShapeDtypeStruct(a.shape, a.dtype) for a in arrays),
        in_specs=[anywhere] * len(arrays),
        out_specs=(anywhere,) * len(arrays),
        scratch_shapes=[pltpu.SemaphoreType.DMA((len(arrays),))],
    )(*arrays)


def solution(mesh):
    in_specs = (
        P("rep", "fsdp", None),
        P("rep", "fsdp", None),
        P("rep", None),
        P("rep", None, "fsdp"),
        P("rep", None, "fsdp"),
        P("rep", "fsdp", None),
        P(),
    )
    out_specs = (
        P("rep", "fsdp", None),
        P("rep", None),
        P("rep", None, "fsdp"),
        P("rep", None, "fsdp"),
        P("rep", "fsdp", None),
    )
    return jax.shard_map(local, mesh=mesh, in_specs=in_specs, out_specs=out_specs, check_vma=False)
```

time: 143 us -> 111 us (0.78); the launches traced: 141 us -> 111 us
  Pallas kernels: 133 us -> 109 us
  local copies, waits for them, and re-layouts: 5.57 us -> 0.68 us
    pallas_call x1, Pallas kernels: 133 us -> 107 us  [step_on_device(): pl.pallas_call(functools.partial(kernel, level), out_shape=(jax.ShapeDtyp...]
    cond x2 -> x0, local copies, waits for them, and re-layouts: 2.61 us -> none  [local(): lax.switch(step_index[0] % level_count, branches, tokens[0], cotangent[0]...]
    unnamed x5 -> x2, local copies, waits for them, and re-layouts: 2.95 us -> 0.68 us
    pallas_call x0 -> x1, Pallas kernels: none -> 1.8 us  [place_results(): pl.pallas_call(body, out_shape=tuple((jax.ShapeDtypeStruct(a.shape, a.dty...]
where the time goes in v2:
time: 111 us
  Pallas kernels  109 us (98%)
  between operations  1.49 us (1%)
    pallas_call x1, Pallas kernels, step_on_device(): pl.pallas_call(functools.partial(kernel, level), out_shape=(jax.ShapeDtyp...  107 us

profile of v2, /device:TPU:16, one launch (start us, length us, event | category | flops | bytes accessed | tf_op | source)
XLA Modules:
  0.0 111.2 jit_solution(12563394788547882769)
XLA Ops:
  1.3 0.0 copy-start
  1.3 0.7 copy-done
  2.0 107.3 %conditional.1 = ((bf16[64,2048]{1,0:T(8,128)(2,1)S(1)}, f32[1,2048]{1,0:T(1,128)S(1)}, f32[2048,128]{1,0:T(8,128)S(1)}, f32[2048,128]{1,0:T(8,128)S(1)}, f32[128,2048]{1,0:T(8,128)S(1)})) conditional(s32[]{:T(128)} %clamp.3, (bf16[64,2048]{1,0:T(8,128)(2,1)}, bf16[64,2048]{1,0:T(8,128)(2,1)}, f32[1,2048]{1,0:T(1,128)S(1)}, ...), branch_computations={%region_0.1_spmd, %region_1.2_spmd, %region_2.3_spmd} | conditional | flops 8589934592 | bytes 8388616 | solution.py:623
  2.0 107.1 %branch_2_fun.1 = (bf16[64,2048]{1,0:T(8,128)(2,1)S(1)}, f32[1,2048]{1,0:T(1,128)S(1)}, f32[2048,128]{1,0:T(8,128)S(1)}, f32[2048,128]{1,0:T(8,128)S(1)}, f32[128,2048]{1,0:T(8,128)S(1)}) custom-call(bf16[64,2048]{1,0:T(8,128)(2,1)} %get-tuple-element.73.tok_hbm, bf16[64,2048]{1,0:T(8,128)(2,1)} %get-tuple-element.74.cot_hbm, ...), custom_call_target="tpu_custom_call" | custom-call | flops 8589934592 | bytes 8388608 | tf_op jit(solution)/shard_map/cond/branch_2_fun/pallas_call | solution.py:555
  109.3 1.8 %shard_map.110 = (bf16[1,64,2048]{2,1,0:T(8,128)(2,1)}, f32[1,2048]{1,0:T(1,128)}, f32[1,2048,128]{2,1,0:T(8,128)}, f32[1,2048,128]{2,1,0:T(8,128)}, f32[1,128,2048]{2,1,0:T(8,128)}) custom-call(bf16[1,64,2048]{2,1,0:T(8,128)(2,1)S(1)} %bitcast.13, f32[1,2048]{1,0:T(1,128)S(1)} %get-tuple-element.118.refs_1_, f32[1,2048,128]{2,1,0:T(8,128)S(1)} %bitcast.10, ...), custom_call_target="tpu_custom_call" | custom-call | tf_op jit(solution)/shard_map/pallas_call | solution.py:644
Async XLA Ops:
  1.3 0.7 copy-start

commit v3 on v2

--- a/solution.py
+++ b/solution.py
@@ -18,8 +18,9 @@
 NN = (((1,), (0,)), ((), ()))
 
 OWN, FOUR = 6, 7
-DEPTH = 3
-WIDTH = 512
+DEPTH = 4
+TILE = 512
+WIDTH = 256
 
 
 def kernel(
@@ -49,6 +50,8 @@
     across = (rep, me + 2 - 4 * lax.rem(me // 2, 2))
     far = 1 << level
     partner = (rep + far - 2 * far * lax.rem(rep // far, 2), me)
+    third = (partner[0], across[1])
+    others = (up, down, sib, across, partner) + ((third,) if level == 0 else ())
     ring = (up, down)
 
     def remote(src, dst, send, recv, device):
@@ -72,9 +75,9 @@
         load.start()
 
     barrier = pltpu.get_barrier_semaphore()
-    for other in (up, down, sib, across, partner):
+    for other in others:
         pl.semaphore_signal(barrier, inc=1, device_id=other, device_id_type=MESH)
-    pl.semaphore_wait(barrier, 5)
+    pl.semaphore_wait(barrier, len(others))
 
     def gather(which, direction, step):
         buffer = (normed, cot)[which]
@@ -179,15 +182,15 @@
             xt[n, cols, lanes_of(g)] = grad.T.astype(BF16)
 
     def term(g):
-        @pl.loop(0, pieces)
+        @pl.loop(0, width // TILE)
         def _(c):
-            part = at_tile(c * WIDTH, WIDTH)
+            part = at_tile(c * TILE, TILE)
             value = lax.dot_general(back[0, g], wb[0, :, part], NN, preferred_element_type=F32)
             value += lax.dot_general(back[1, g], wb[1, :, part], NN, preferred_element_type=F32)
             value = value * in_scale
-            terms[pl.ds(2 * g, 2), :, part] = value.astype(BF16).reshape(2, rows, WIDTH)
-            along = value * normed[pl.ds(2 * g, 2), :, part].reshape(2 * rows, WIDTH).astype(F32)
-            gain_one[0, :, part] += jnp.sum(along.reshape(rows // 4, 8, WIDTH), axis=0)
+            terms[pl.ds(2 * g, 2), :, part] = value.astype(BF16).reshape(2, rows, TILE)
+            along = value * normed[pl.ds(2 * g, 2), :, part].reshape(2 * rows, TILE).astype(F32)
+            gain_one[0, :, part] += jnp.sum(along.reshape(rows // 4, 8, TILE), axis=0)
 
     gain_one[0] = jnp.zeros((8, width), F32)
 
@@ -255,46 +258,37 @@
         def _(g):
             forward(g, 1)
 
-    for direction in (0, 1):
-        gather_half(1, direction).wait_recv()
-
-    def scatter_first(direction):
-        part = pl.ds(direction * half, half)
+    def scatter_send(direction, chain, step):
+        part = pl.ds(((direction + chain) % 2) * half, half)
+        slot = 2 * (step - 1) + 1 - direction
+        if step == 4:
+            src = terms.at[FOUR, part]
+        elif step == 3 and chain == 1:
+            src = terms.at[slot, part]
+        else:
+            src = rs_out.at[direction, 3 - step, part]
         return remote(
-            terms.at[FOUR, part], rs_in.at[direction, 0, part],
-            rs_s.at[direction, 0], rs_r.at[direction, 0], ring[direction],
-        )
-
-    def scatter_send(direction, step):
-        return remote(
-            rs_out.at[direction, 3 - step], rs_in.at[direction, 4 - step],
-            rs_s.at[direction, 4 - step], rs_r.at[direction, 4 - step], ring[direction],
-        )
-
-    def scatter_step(step):
+            src, rs_in.at[direction, 4 - step, part],
+            rs_s.at[direction, chain, 4 - step], rs_r.at[direction, chain, 4 - step],
+            ring[direction],
+        )
+
+    def scatter_step(chain, step):
         for direction in (0, 1):
-            if step == 3:
-                scatter_first(direction).wait_recv()
-            else:
-                scatter_send(direction, step + 1).wait_recv()
+            scatter_send(direction, chain, step + 1).wait_recv()
             slot = 2 * (step - 1) + 1 - direction
-
-            @pl.loop(0, rows // 16)
-            def _(r):
-                part = at_tile(r * 16, 16)
+            start = ((direction + chain) % 2) * half
+            for r in range(start, start + half, 16):
+                part = slice(r, r + 16)
                 value = terms[slot, part, :].astype(F32)
-                if step == 3:
-                    inside = (r // (half // 16)) == direction
-                    came = jnp.where(inside, rs_in[direction, 0, part, :].astype(F32), 0.0)
-                else:
-                    came = rs_in[direction, 3 - step, part, :].astype(F32)
+                came = rs_in[direction, 3 - step, part, :].astype(F32)
                 rs_out[direction, 3 - step, part, :] = (value + came).astype(BF16)
-
-            scatter_send(direction, step).start()
+            scatter_send(direction, chain, step).start()
 
     def scatter_last():
         for direction in (0, 1):
-            scatter_send(direction, 1).wait_recv()
+            for chain in (0, 1):
+                scatter_send(direction, chain, 1).wait_recv()
         @pl.loop(0, rows // 16)
         def _(r):
             part = at_tile(r * 16, 16)
@@ -379,8 +373,18 @@
     def sib_copy(i):
         return remote(sib_out.at[i], sib_in.at[i], sib_s.at[i], sib_r.at[i], sib)
 
-    def y_copy(i):
-        return remote(y_out.at[i], y_in.at[i], y_s.at[i], y_r.at[i], across)
+    def y_copies(i):
+        if level > 0:
+            return (remote(y_out.at[i], y_in.at[i], y_s.at[0, i], y_r.at[0, i], across),)
+        side = lax.rem(rep, 2)
+        return (
+            remote(y_out.at[i, side], y_in.at[i, 0], y_s.at[0, i], y_r.at[0, i], across),
+            remote(y_out.at[i, 1 - side], y_in.at[i, 1], y_s.at[1, i], y_r.at[1, i], third),
+        )
+
+    def y_start(i):
+        for copy in y_copies(i):
+            copy.start()
 
     def x_copy(i):
         return remote(x_out.at[i], x_in.at[i], x_s.at[i], x_r.at[i], partner)
@@ -398,20 +402,30 @@
 
     def add_sib(i):
         sib_copy(i).wait_recv()
-        y_out[i] = (keep[i, 1] + sib_in[i, 1].astype(F32)).astype(BF16)
+        value = (keep[i, 1] + sib_in[i, 1].astype(F32)).astype(BF16)
+        y_out[i, 0] = value[:, :WIDTH // 2]
+        y_out[i, 1] = value[:, WIDTH // 2:]
         keep[i, 0] += sib_in[i, 0].astype(F32)
 
     def add_across(i):
         m, cols = piece(i)
-        y_copy(i).wait_recv()
-        new = wt[m, :, cols] - learn_rate * (keep[i, 0] + y_in[i].astype(F32))
+        for copy in y_copies(i):
+            copy.wait_recv()
+        if level > 0:
+            parts = [y_in[i, n].astype(F32) for n in (0, 1)]
+        else:
+            came = y_in[i, 0].astype(F32) + y_in[i, 1].astype(F32)
+            side = lax.rem(rep, 2)
+            parts = [jnp.where(side == n, came, 0.0) for n in (0, 1)]
+        total = keep[i, 0] + jnp.concatenate(parts, axis=1)
+        new = wt[m, :, cols] - learn_rate * total
         keep[i, 0] = new
         x_out[i] = new.astype(BF16)
         x_copy(i).start()
 
         @pl.when(i < count - DEPTH)
         def _():
-            y_copy(i + DEPTH).start()
+            y_start(i + DEPTH)
 
     def write(target, i):
         m, cols = piece(i)
@@ -441,68 +455,76 @@
         def _():
             write_turned(nu_out, i).start()
 
-    @pl.loop(0, pieces)
+    for direction in (0, 1):
+        gather_half(1, direction).wait_recv()
+
+    @pl.loop(0, pieces + 1)
     def _(i):
-        product(i, 2, cot, out_scale)
+        @pl.when(i < pieces)
+        def _():
+            product(i, 2, cot, out_scale)
+
+        @pl.when(i > 0)
+        def _():
+            add_sib(i - 1)
+
+        @pl.when((i > 0) & (i <= DEPTH))
+        def _():
+            y_start(i - 1)
 
     weight_passed(2).wait_recv()
 
     @pl.loop(0, 5)
     def _(j):
         last = 2 // (j + 1) - 1 // (j + 1)
-        backward(3 * last + (j - 2) * (1 - last), 1 - 1 // (j + 1))
-
-        @pl.when(j < pieces)
-        def _():
-            add_sib(j)
-
-        @pl.when(j < DEPTH)
-        def _():
-            y_copy(j).start()
+        g = 3 * last + (4 - j) * (1 - last)
+        backward(g, 1 - 1 // (j + 1))
+
+        @pl.when(j > 0)
+        def _():
+            term(g)
 
         @pl.when(j == 1)
         def _():
-            term(3)
-            for direction in (0, 1):
-                scatter_first(direction).start()
-
-    @pl.loop(pieces, count)
+            for direction in (0, 1):
+                scatter_send(direction, 0, 4).start()
+
+        @pl.when(j == 2)
+        def _():
+            for direction in (0, 1):
+                scatter_send(direction, 1, 3).start()
+
+        @pl.when(j > 1)
+        def _():
+            add_across(j - 2)
+
+    gain_sib()
+
+    extra = {
+        3: lambda: scatter_step(0, 3),
+        4: gain_across,
+        5: lambda: scatter_step(1, 2),
+        7: lambda: scatter_step(0, 2),
+        9: lambda: scatter_step(1, 1),
+        10: gain_ring_start,
+        11: lambda: scatter_step(0, 1),
+        16: lambda: (scatter_last(), gain_ring_step(2)),
+        18: lambda: gain_ring_step(3),
+        20: lambda: gain_ring_step(4),
+        22: gain_finish,
+    }
+
+    @pl.loop(3, count + 3)
     def _(i):
-        m, _cols = piece(i)
-        product(i, m, normed, in_scale)
-
-        @pl.when(i > pieces)
-        def _():
-            add_sib(i - 1)
-
-        @pl.when(i < pieces + 3)
-        def _():
-            term(2 + pieces - i)
-
-        @pl.when(i == pieces + 3)
-        def _():
-            scatter_step(3)
-            gain_sib()
-
-        for p, at in enumerate((pieces + 2, pieces + 5)):
-            @pl.when(i == at)
-            def _():
-                add_across(p)
-
-    add_sib(count - 1)
-
-    extra = {
-        2: gain_across,
-        3: gain_ring_start,
-        4: lambda: (scatter_step(2), gain_ring_step(2)),
-        5: lambda: gain_ring_step(3),
-        6: lambda: gain_ring_step(4),
-        7: lambda: (scatter_step(1), gain_finish()),
-        10: scatter_last,
-    }
-
-    @pl.loop(2, count + 2)
-    def _(i):
+        @pl.when(i < count - DEPTH - 1)
+        def _():
+            m, _cols = piece(i + DEPTH + 1)
+            product(i + DEPTH + 1, m, normed, in_scale)
+
+        @pl.when((i > 3) & (i < count - DEPTH))
+        def _():
+            add_sib(i + DEPTH)
+
         @pl.when(i < count)
         def _():
             add_across(i)
@@ -512,7 +534,7 @@
             def _():
                 action()
 
-        average(i - 2)
+        average(i - 3)
 
     gain_average()
 
@@ -525,9 +547,9 @@
         for copy in (weight_across, weight_sib, weight_passed):
             copy(m).wait_send()
     for direction in (0, 1):
-        scatter_first(direction).wait_send()
-        for step in (3, 2, 1):
-            scatter_send(direction, step).wait_send()
+        for chain in (0, 1):
+            for step in (4, 3, 2, 1)[chain:]:
+                scatter_send(direction, chain, step).wait_send()
     for name in ("sib", "across", "partner"):
         gain_copy(name).wait_send()
     for step in (1, 2, 3, 4):
@@ -538,7 +560,8 @@
     @pl.loop(0, count)
     def _(i):
         sib_copy(i).wait_send()
-        y_copy(i).wait_send()
+        for copy in y_copies(i):
+            copy.wait_send()
         x_copy(i).wait_send()
         write(nd_out, i).wait()
 
@@ -577,8 +600,8 @@
             pltpu.VMEM((count, 2, units, WIDTH), BF16),
             pltpu.VMEM((count, 2, units, WIDTH), BF16),
             pltpu.VMEM((count, 2, units, WIDTH), F32),
-            pltpu.VMEM((count, units, WIDTH), BF16),
-            pltpu.VMEM((count, units, WIDTH), BF16),
+            pltpu.VMEM((count, 2, units, WIDTH // 2), BF16),
+            pltpu.VMEM((count, 2, units, WIDTH // 2), BF16),
             pltpu.VMEM((count, units, WIDTH), BF16),
             pltpu.VMEM((count, units, WIDTH), BF16),
             pltpu.VMEM((2, 3, rows, width), BF16),
@@ -599,12 +622,12 @@
             dma((3, 3)),
             dma((count,)),
             dma((count,)),
+            dma((2, count)),
+            dma((2, count)),
             dma((count,)),
             dma((count,)),
-            dma((count,)),
-            dma((count,)),
-            dma((2, 4)),
-            dma((2, 4)),
+            dma((2, 2, 4)),
+            dma((2, 2, 4)),
             dma((10,)),
             dma((10,)),
         ],

time: 111 us -> 108 us (0.973)
  Pallas kernels: 109 us -> 105 us
    pallas_call x1, Pallas kernels: 107 us -> 104 us  [step_on_device(): pl.pallas_call(functools.partial(kernel, level), out_shape=(jax.ShapeDtyp...]
where the time goes in v3:
time: 108 us
  Pallas kernels  105 us (97%)
  between operations  1.49 us (1%)
    pallas_call x1, Pallas kernels, step_on_device(): pl.pallas_call(functools.partial(kernel, level), out_shape=(jax.ShapeDtyp...  104 us

profile of v3, /device:TPU:16, one launch (start us, length us, event | category | flops | bytes accessed | tf_op | source)
XLA Modules:
  0.0 107.7 jit_solution(8482685649314936895)
XLA Ops:
  1.3 0.0 copy-start
  1.3 0.7 copy-done
  2.0 103.7 %conditional.1 = ((bf16[64,2048]{1,0:T(8,128)(2,1)S(1)}, f32[1,2048]{1,0:T(1,128)S(1)}, f32[2048,128]{1,0:T(8,128)S(1)}, f32[2048,128]{1,0:T(8,128)S(1)}, f32[128,2048]{1,0:T(8,128)S(1)})) conditional(s32[]{:T(128)} %clamp.3, (bf16[64,2048]{1,0:T(8,128)(2,1)}, bf16[64,2048]{1,0:T(8,128)(2,1)}, f32[1,2048]{1,0:T(1,128)S(1)}, ...), branch_computations={%region_0.1_spmd, %region_1.2_spmd, %region_2.3_spmd} | conditional | flops 8589934592 | bytes 8388616 | solution.py:646
  2.0 103.5 %branch_2_fun.1 = (bf16[64,2048]{1,0:T(8,128)(2,1)S(1)}, f32[1,2048]{1,0:T(1,128)S(1)}, f32[2048,128]{1,0:T(8,128)S(1)}, f32[2048,128]{1,0:T(8,128)S(1)}, f32[128,2048]{1,0:T(8,128)S(1)}) custom-call(bf16[64,2048]{1,0:T(8,128)(2,1)} %get-tuple-element.73.tok_hbm, bf16[64,2048]{1,0:T(8,128)(2,1)} %get-tuple-element.74.cot_hbm, ...), custom_call_target="tpu_custom_call" | custom-call | flops 8589934592 | bytes 8388608 | tf_op jit(solution)/shard_map/cond/branch_2_fun/pallas_call | solution.py:578
  105.7 1.8 %shard_map.110 = (bf16[1,64,2048]{2,1,0:T(8,128)(2,1)}, f32[1,2048]{1,0:T(1,128)}, f32[1,2048,128]{2,1,0:T(8,128)}, f32[1,2048,128]{2,1,0:T(8,128)}, f32[1,128,2048]{2,1,0:T(8,128)}) custom-call(bf16[1,64,2048]{2,1,0:T(8,128)(2,1)S(1)} %bitcast.13, f32[1,2048]{1,0:T(1,128)S(1)} %get-tuple-element.118.refs_1_, f32[1,2048,128]{2,1,0:T(8,128)S(1)} %bitcast.10, ...), custom_call_target="tpu_custom_call" | custom-call | tf_op jit(solution)/shard_map/pallas_call | solution.py:667
Async XLA Ops:
  1.3 0.7 copy-start
